TPU v7x, 256 devices: a whole 4x4x8 slice. The times are simulated.
256 devices in a mesh: row: 32 (over y, z), col: 8 (over x, core).
Axes of the slice: x: 4, y: 4, z: 8, core: 2. Of those that a mesh axis runs over, the one named last changes fastest.
Arguments:
- param_up: float32 [4096, 16384], P('row', 'col'), may hold values from -0.09375 to 0.09375
- grad_up: bfloat16 [4096, 16384], P('row', 'col'), as said below
- mom_up: bfloat16 [4096, 16384], P('row', 'col'), may hold values from -6 to 6
- rows_up: float32 [4096], P('row'), may hold values from 500 to 45000, as said below
- cols_up: float32 [16384], P('col'), may hold values from 0.5 to 5000
- param_attn: float32 [4096, 4096], P('row', 'col'), may hold values from -0.09375 to 0.09375
- grad_attn: bfloat16 [4096, 4096], P('row', 'col'), as said below
- mom_attn: bfloat16 [4096, 4096], P('row', 'col'), may hold values from -6 to 6
- rows_attn: float32 [4096], P('row'), may hold values from 500 to 45000, as said below
- cols_attn: float32 [4096], P('col'), may hold values from 0.5 to 5000
Outputs:
- new_param_up: float32 [4096, 16384], P('row', 'col')
- new_mom_up: bfloat16 [4096, 16384], P('row', 'col')
- new_rows_up: float32 [4096], P('row')
- new_cols_up: float32 [16384], P('col')
- copy_up: bfloat16 [4096, 16384], P('row')
- new_param_attn: float32 [4096, 4096], P('row', 'col')
- new_mom_attn: bfloat16 [4096, 4096], P('row', 'col')
- new_rows_attn: float32 [4096], P('row')
- new_cols_attn: float32 [4096], P('col')
- copy_attn: bfloat16 [4096, 4096], P('row')
- mean_logs: float32 [4], replicated
Inputs may be any that keep to these rules, and one draw needn't show every extreme that they name: `grad_up`: finite gradient entries. `grad_attn`: finite gradient entries. `rows_up`: positive entries. `rows_attn`: positive entries.
All inputs are finite; a program needn't handle non-finite values.
Results may differ from a plain program's by a relative error of at most 0.0075.
Values may be sent and summed in bfloat16 or wider, within the bound.
A program may use at most 64 MiB of HBM per device.

v0:
```python
import jax
import jax.numpy as jnp
from jax import lax
from jax.sharding import PartitionSpec as P

D = 4096
FF = 16384


DECAY = 0.8415
BETA = 0.9
RATE = 0.01
TINY = 1e-30


def advance(param, wide, mom, new_rows, new_cols, row_mean, clip):
    update = wide / jnp.sqrt(new_rows[:, None] * new_cols[None, :] / row_mean)
    new_mom = (BETA * mom.astype(jnp.float32) + (1.0 - BETA) * clip * update).astype(jnp.bfloat16)
    new_param = param - RATE * new_mom.astype(jnp.float32)
    return (new_param, new_mom, new_param.astype(jnp.bfloat16))


def normed(wide, new_rows, new_cols, row_mean):
    update = wide / jnp.sqrt(new_rows[:, None] * new_cols[None, :] / row_mean)
    return jnp.sum(update * update)


def on_device(
    param_up,
    grad_up,
    mom_up,
    rows_up,
    cols_up,
    param_attn,
    grad_attn,
    mom_attn,
    rows_attn,
    cols_attn,
):
    wide_up = grad_up.astype(jnp.float32)
    wide_attn = grad_attn.astype(jnp.float32)
    sq_up = wide_up * wide_up + TINY
    sq_attn = wide_attn * wide_attn + TINY
    part_rows_up = jnp.sum(sq_up, axis=1)
    part_rows_attn = jnp.sum(sq_attn, axis=1)
    full_rows = lax.psum((part_rows_up, part_rows_attn), "col")
    full_cols = lax.psum((jnp.sum(sq_up, axis=0), jnp.sum(sq_attn, axis=0)), "row")
    new_rows_up = DECAY * rows_up + (1.0 - DECAY) * full_rows[0] / FF
    new_rows_attn = DECAY * rows_attn + (1.0 - DECAY) * full_rows[1] / D
    new_cols_up = DECAY * cols_up + (1.0 - DECAY) * full_cols[0] / D
    new_cols_attn = DECAY * cols_attn + (1.0 - DECAY) * full_cols[1] / D
    sums = lax.psum((jnp.sum(new_rows_up), jnp.sum(new_rows_attn)), "row")
    mean_up = sums[0] / D
    mean_attn = sums[1] / D
    squares = lax.psum(
        (
            normed(wide_up, new_rows_up, new_cols_up, mean_up),
            normed(wide_attn, new_rows_attn, new_cols_attn, mean_attn),
        ),
        ("row", "col"),
    )
    square_up = squares[0] / (D * FF)
    square_attn = squares[1] / (D * D)
    mean_logs = jnp.stack(
        [jnp.log(mean_up), jnp.log(mean_attn), jnp.log(square_up), jnp.log(square_attn)]
    )
    clip_up = 1.0 / jnp.maximum(1.0, jnp.sqrt(square_up))
    clip_attn = 1.0 / jnp.maximum(1.0, jnp.sqrt(square_attn))
    param_new_up, mom_new_up, lowered_up = advance(
        param_up, wide_up, mom_up, new_rows_up, new_cols_up, mean_up, clip_up
    )
    param_new_attn, mom_new_attn, lowered_attn = advance(
        param_attn, wide_attn, mom_attn, new_rows_attn, new_cols_attn, mean_attn, clip_attn
    )
    copy_up, copy_attn = (
        lax.all_gather(lowered_up, "col", axis=1, tiled=True),
        lax.all_gather(lowered_attn, "col", axis=1, tiled=True),
    )
    return (
        param_new_up,
        mom_new_up,
        new_rows_up,
        new_cols_up,
        copy_up,
        param_new_attn,
        mom_new_attn,
        new_rows_attn,
        new_cols_attn,
        copy_attn,
        mean_logs,
    )


def solution(mesh):
    in_specs = (
        P("row", "col"),
        P("row", "col"),
        P("row", "col"),
        P("row"),
        P("col"),
        P("row", "col"),
        P("row", "col"),
        P("row", "col"),
        P("row"),
        P("col"),
    )
    out_specs = (
        P("row", "col"),
        P("row", "col"),
        P("row"),
        P("col"),
        P("row", None),
        P("row", "col"),
        P("row", "col"),
        P("row"),
        P("col"),
        P("row", None),
        P(),
    )
    return jax.shard_map(
        on_device, mesh=mesh, in_specs=in_specs, out_specs=out_specs, check_vma=False
    )
```

profile of v0, /device:TPU:1, one launch (start us, length us, event | category | flops | bytes accessed | tf_op | source)
XLA Modules:
  0.0 323.8 jit_solution(8915311796894249760)
XLA Ops:
  7.2 0.0 all-gather.5.cloned.1.call-start
  7.2 1.3 fusion.1
  8.5 1.0 fusion.4
  9.5 15.0 %all-reduce.2 = (f32[128]{0:T(128)S(1)}, f32[128]{0:T(128)S(1)}) all-reduce(f32[128]{0:T(128)S(1)} %get-tuple-element.12, f32[128]{0:T(128)S(1)} %get-tuple-element.14), channel_id=1, replica_groups=mesh['row'=32,'col'=8] {'col'}, use_global_device_ids=true, to_apply=%region_1.0 | all-reduce | flops 256 | bytes 2048 | tf_op jit(solution)/shard_map/psum | solution.py:46
  24.6 1.3 fusion.8
  25.8 0.0 copy-start.3
  25.8 0.0 copy-start.4
  25.8 116.8 %all-reduce.1 = (f32[]{:T(128)}, f32[2048]{0:T(1024)S(1)}, f32[]{:T(128)}, f32[512]{0:T(512)S(1)}) all-reduce(f32[]{:T(128)} %get-tuple-element.33, f32[2048]{0:T(1024)S(1)} %get-tuple-element.11, f32[]{:T(128)} %get-tuple-element.29, f32[512]{0:T(512)S(1)} %get-tuple-element.13), channel_id=1, replica_groups=mesh['row'=32,'col'=8] {'row'}, use_global_device_ids=true, to_apply=%region_5.0 | all-reduce | flops 2562 | bytes 20496 | tf_op jit(solution)/shard_map/psum | solution.py:52
  143.9 0.7 multiply_add_fusion
  144.7 0.0 copy-start.1
  144.7 0.7 multiply_add_fusion.1
  145.3 0.0 copy-start.2
  145.3 2.0 multiply_reduce_fusion
  147.3 1.7 multiply_reduce_fusion.1
  149.0 100.8 %all-reduce = (f32[]{:T(128)}, f32[]{:T(128)}) all-reduce(f32[]{:T(128)} %multiply_reduce_fusion, f32[]{:T(128)} %multiply_reduce_fusion.1), channel_id=1, replica_groups=mesh['row'=32,'col'=8] {'row','col'}, use_global_device_ids=true, to_apply=%region_7.0 | all-reduce | flops 2 | bytes 16 | tf_op jit(solution)/shard_map/psum | solution.py:55
  250.5 2.0 fusion.6
  252.5 0.0 all-gather.5.cloned.1.call-update
  252.6 0.0 all-gather.3.cloned.1.call-start
  253.3 3.3 %fusion.7 = (bf16[128,2048]{1,0:T(8,128)(2,1)}, f32[128,2048]{1,0:T(8,128)}, bf16[128,2048]{1,0:T(8,128)(2,1)}) fusion(f32[128,2048]{1,0:T(8,128)} %param.10, f32[]{:T(128)S(6)} %div.70, f32[2048]{0:T(1024)S(1)} %multiply_add_fusion, f32[128]{0:T(128)S(1)} %get-tuple-element.48, bf16[128,2048]{1,0:T(8,128)(2,1)} %param.11, f32[]{:T(128)S(6)} %mul.128, ...), kind=kLoop, calls=%fused_computation.22 | loop fusion | flops 3407872 | bytes 4203016 | tf_op jit(solution)/shard_map/convert_element_type | solution.py:20
  256.7 0.0 all-gather.3.cloned.1.call-update
  256.9 0.6 pad_maximum_fusion
  257.4 16.9 %all-gather.5.cloned.1.call-done = bf16[128,4096]{1,0:T(8,128)(2,1)} async-done(((bf16[128,512]{1,0:T(8,128)(2,1)}), bf16[128,4096]{1,0:T(8,128)(2,1)}) %all-gather.5.cloned.1.call-update) | async-done | bytes 1048592 | tf_op jit(solution)/shard_map/all_gather | solution.py:77
  274.3 37.0 %all-gather.3.cloned.1.call-done = bf16[128,16384]{1,0:T(8,128)(2,1)} async-done(((bf16[128,2048]{1,0:T(8,128)(2,1)}), bf16[128,16384]{1,0:T(8,128)(2,1)}) %all-gather.3.cloned.1.call-update) | async-done | bytes 4194320 | tf_op jit(solution)/shard_map/all_gather | solution.py:76
  311.3 0.0 copy-start
  311.3 4.7 %copy.23 = bf16[128,16384]{1,0:T(8,128)(2,1)} copy(bf16[128,16384]{1,0:T(8,128)(2,1)} %all-gather.3.cloned.1.call-done) | data formatting | bytes 8388608
  316.0 0.0 copy-done.3
  316.0 0.0 copy-done.4
  316.0 0.0 copy-done.1
  316.0 0.0 copy-done.2
  316.0 0.0 copy-done
  316.0 1.0 copy.24
Async XLA Ops:
  7.2 267.1 %all-gather.5.cloned.1.call-start = ((), (), s32[]{:S(2)}) async-start(), calls=%async_computation.1 | async-start | bytes 1179648 | tf_op jit(solution)/shard_map/all_gather | solution.py:77
  25.8 290.1 %copy-start.3 = (f32[128]{0:T(128)}, f32[128]{0:T(128)S(1)}, u32[]{:S(2)}) copy-start(f32[128]{0:T(128)S(1)} %get-tuple-element.53) | copy-start | bytes 1540
  25.8 290.1 %copy-start.4 = (f32[128]{0:T(128)}, f32[128]{0:T(128)S(1)}, u32[]{:S(2)}) copy-start(f32[128]{0:T(128)S(1)} %get-tuple-element.48) | copy-start | bytes 1540
  144.7 171.3 %copy-start.1 = (f32[2048]{0:T(1024)}, f32[2048]{0:T(1024)S(1)}, u32[]{:S(2)}) copy-start(f32[2048]{0:T(1024)S(1)} %multiply_add_fusion) | copy-start | bytes 24580
  145.3 170.6 %copy-start.2 = (f32[512]{0:T(512)}, f32[512]{0:T(512)S(1)}, u32[]{:S(2)}) copy-start(f32[512]{0:T(512)S(1)} %multiply_add_fusion.1) | copy-start | bytes 6148
  252.6 58.8 %all-gather.3.cloned.1.call-start = ((), (), s32[]{:S(2)}) async-start(), calls=%async_computation | async-start | bytes 4718592 | tf_op jit(solution)/shard_map/all_gather | solution.py:76
  311.3 4.7 %copy-start = (bf16[128,4096]{1,0:T(8,128)(2,1)S(1)}, bf16[128,4096]{1,0:T(8,128)(2,1)}, u32[]{:S(2)}) copy-start(bf16[128,4096]{1,0:T(8,128)(2,1)} %all-gather.5.cloned.1.call-done) | copy-start | bytes 3145732
Sparse Core Ops, SparseCore 0:
  252.7 21.6 all-gather.4
  276.7 34.5 all-gather.2
where the time goes:
time: 324 us
  blocking collectives  233 us (72%)
  waiting for transfers between devices  53.9 us (17%)
  between operations  17 us (5%)
  other arithmetic  14.6 us (5%)
  local copies, waits for them, and re-layouts  5.65 us (2%)
    psum x1, blocking collectives, on_device(): sums = lax.psum((jnp.sum(new_rows_up), jnp.sum(new_rows_attn)), 'row')  117 us
    psum x1, blocking collectives, on_device(): lax.psum((normed(wide_up, new_rows_up, new_cols_up, mean_up), normed(wide...  101 us
    all_gather x1, waiting for transfers between devices, on_device(): lax.all_gather(lowered_up, 'col', axis=1, tiled=True)  37 us
    all_gather x1, waiting for transfers between devices, on_device(): lax.all_gather(lowered_attn, 'col', axis=1, tiled=True)  16.9 us
    psum x1, blocking collectives, on_device(): full_rows = lax.psum((part_rows_up, part_rows_attn), 'col')  15 us
  transfers between devices with their start and end apart: 2, of which 2 were waited for; matrix products, arithmetic and copies ran while one was open for 1% of the time, Pallas kernels for 0%

commit v1 on v0

v1 whole, which is shorter than its diff:
```python
import functools

import jax
import jax.numpy as jnp
from jax import lax
from jax.experimental import pallas as pl
from jax.experimental.pallas import tpu as pltpu
from jax.sharding import PartitionSpec as P

DECAY = 0.8415
BETA = 0.9
RATE = 0.01
TINY = 1e-30

MESH = pl.DeviceIdType.MESH
F32 = jnp.float32
BF16 = jnp.bfloat16


def body(
    dims,
    p_up, g_up, m_up, r_up, c_up, p_at, g_at, m_at, r_at, c_at,
    np_up, nm_up, nr_up, nc_up, cp_up, np_at, nm_at, nr_at, nc_at, cp_at, logs,
    vg_up, vg_at, vm_up, vm_at, vp_up, vp_at, vr, vc,
    lane_part, rs, cs_y, cs_z, tt_y, tt_z, sq, in_sem,
    rs_send, rs_recv, cy_send, cy_recv, cz_send, cz_recv,
    ty_send, ty_recv, tz_send, tz_recv, sq_send, sq_recv,
    own_send, near_recv, far_send, far_recv, sib_send, sib_recv,
):
    ny, nz, nx = dims
    n_col = 2 * nx
    rows, cu = g_up.shape
    ca = g_at.shape[1]
    cw = cu + ca
    n_rows = rows * ny * nz
    full_up = cu * n_col
    full_at = ca * n_col

    row = lax.axis_index("row")
    col = lax.axis_index("col")
    y, z = row // nz, row % nz
    x, core = col // 2, col % 2

    col_peers = [lax.rem(col + k, n_col) for k in range(1, n_col)]
    y_peers = [lax.rem(y + k, ny) for k in range(1, ny)]
    z_peers = [lax.rem(z + k, nz) for k in range(1, nz)]

    barrier = pltpu.get_barrier_semaphore()
    for c in col_peers:
        pl.semaphore_signal(barrier, inc=1, device_id=(row, c), device_id_type=MESH)
    for q in y_peers:
        pl.semaphore_signal(barrier, inc=1, device_id=(q * nz + z, col), device_id_type=MESH)
    for q in z_peers:
        pl.semaphore_signal(barrier, inc=1, device_id=(y * nz + q, col), device_id_type=MESH)

    loads = [
        pltpu.make_async_copy(src, dst, in_sem.at[i])
        for i, (src, dst) in enumerate(
            [
                (g_up, vg_up),
                (g_at, vg_at),
                (r_up, vr.at[:, pl.ds(0, rows)]),
                (r_at, vr.at[:, pl.ds(rows, rows)]),
                (c_up, vc.at[:, pl.ds(0, cu)]),
                (c_at, vc.at[:, pl.ds(cu, ca)]),
                (m_up, vm_up),
                (p_up, vp_up),
                (m_at, vm_at),
                (p_at, vp_at),
            ]
        )
    ]
    for copy in loads:
        copy.start()

    loads[0].wait()
    loads[1].wait()
    step = 16
    acc = jnp.zeros((8, cw), F32)
    for r0 in range(0, rows, step):
        wide_u = vg_up[r0 : r0 + step, :].astype(F32)
        wide_a = vg_at[r0 : r0 + step, :].astype(F32)
        su = wide_u * wide_u + TINY
        sa = wide_a * wide_a + TINY
        both = jnp.concatenate([su, sa], axis=1)
        for s in range(0, step, 8):
            acc = acc + both[s : s + 8, :]
        lane_part[r0 : r0 + step, :] = functools.reduce(
            jnp.add, [su[:, k : k + 128] for k in range(0, cu, 128)]
        )
        lane_part[rows + r0 : rows + r0 + step, :] = functools.reduce(
            jnp.add, [sa[:, k : k + 128] for k in range(0, ca, 128)]
        )
    cs_y[y] = jnp.sum(acc, axis=0, keepdims=True)

    eye = lax.broadcasted_iota(jnp.int32, (rows, rows), 0) == lax.broadcasted_iota(
        jnp.int32, (rows, rows), 1
    )

    def to_lanes(column):
        return jnp.sum(jnp.where(eye, column, 0.0), axis=0, keepdims=True)

    def to_column(lanes):
        return jnp.sum(jnp.where(eye, lanes, 0.0), axis=1, keepdims=True)

    sums = jnp.sum(lane_part[...], axis=1, keepdims=True)
    rs[col] = jnp.concatenate([to_lanes(sums[:rows]), to_lanes(sums[rows:])], axis=1)

    pl.semaphore_wait(barrier, (n_col - 1) + (ny - 1) + (nz - 1))

    def spread(buf, slot, targets, peers, send, recv):
        out = []
        for k, (dev, peer) in enumerate(zip(targets, peers)):
            copy = pltpu.make_async_remote_copy(
                src_ref=buf.at[slot],
                dst_ref=buf.at[slot],
                send_sem=send.at[k],
                recv_sem=recv.at[slot],
                device_id=dev,
                device_id_type=MESH,
            )
            copy.start()
            out.append(copy)
        return out

    def arrive(buf, peers, recv, send):
        for peer in peers:
            pltpu.make_async_remote_copy(
                src_ref=buf.at[peer],
                dst_ref=buf.at[peer],
                send_sem=send.at[0],
                recv_sem=recv.at[peer],
                device_id=(row, col_peers[0]),
                device_id_type=MESH,
            ).wait_recv()

    def total(buf, n):
        return functools.reduce(jnp.add, [buf[k] for k in range(n)])

    col_devs = [(row, c) for c in col_peers]
    y_devs = [(q * nz + z, col) for q in y_peers]
    z_devs = [(y * nz + q, col) for q in z_peers]
    sent = []
    sent += spread(rs, col, col_devs, col_peers, rs_send, rs_recv)
    sent += spread(cs_y, y, y_devs, y_peers, cy_send, cy_recv)

    for k in range(2, 6):
        loads[k].wait()
    arrive(rs, col_peers, rs_recv, rs_send)
    full_rows = total(rs, n_col)
    old = vr[...]
    lane = lax.broadcasted_iota(jnp.int32, (1, 2 * rows), 1)
    width = jnp.where(lane < rows, 1.0 / full_up, 1.0 / full_at)
    new_rows = DECAY * old + (1.0 - DECAY) * (full_rows * width)
    nr_up[...] = new_rows[:, :rows]
    nr_at[...] = new_rows[:, rows:]
    nr_col_up = to_column(new_rows[:, :rows])
    nr_col_at = to_column(new_rows[:, rows:])
    inv_up = 1.0 / nr_col_up
    inv_at = 1.0 / nr_col_at

    acc = jnp.zeros((8, cw), F32)
    for r0 in range(0, rows, step):
        wide_u = vg_up[r0 : r0 + step, :].astype(F32)
        wide_a = vg_at[r0 : r0 + step, :].astype(F32)
        su = wide_u * wide_u * inv_up[r0 : r0 + step, :]
        sa = wide_a * wide_a * inv_at[r0 : r0 + step, :]
        both = jnp.concatenate([su, sa], axis=1)
        for s in range(0, step, 8):
            acc = acc + both[s : s + 8, :]
    tt_y[y] = jnp.concatenate([jnp.sum(acc, axis=0, keepdims=True), new_rows], axis=1)
    sent += spread(tt_y, y, y_devs, y_peers, ty_send, ty_recv)

    arrive(cs_y, y_peers, cy_recv, cy_send)
    cs_z[z] = total(cs_y, ny)
    sent += spread(cs_z, z, z_devs, z_peers, cz_send, cz_recv)

    arrive(tt_y, y_peers, ty_recv, ty_send)
    tt_z[z] = total(tt_y, ny)
    sent += spread(tt_z, z, z_devs, z_peers, tz_send, tz_recv)

    arrive(cs_z, z_peers, cz_recv, cz_send)
    new_cols = DECAY * vc[...] + (1.0 - DECAY) * (total(cs_z, nz) * (1.0 / n_rows))
    nc_up[...] = new_cols[:, :cu]
    nc_at[...] = new_cols[:, cu:]
    inv_cols = 1.0 / new_cols
    root_cols = lax.rsqrt(new_cols)
    root_up = lax.rsqrt(nr_col_up)
    root_at = lax.rsqrt(nr_col_at)

    arrive(tt_z, z_peers, tz_recv, tz_send)
    tt = total(tt_z, nz)
    terms = tt[:, :cw] * inv_cols
    fold = lambda v: functools.reduce(
        jnp.add, [v[:, k : k + 128] for k in range(0, v.shape[1], 128)]
    )
    sq[col] = jnp.concatenate([fold(terms[:, :cu]), fold(terms[:, cu:])], axis=1)
    sent += spread(sq, col, col_devs, col_peers, sq_send, sq_recv)
    mean_up = jnp.sum(tt[:, cw : cw + rows], axis=1, keepdims=True) * (1.0 / n_rows)
    mean_at = jnp.sum(tt[:, cw + rows :], axis=1, keepdims=True) * (1.0 / n_rows)
    for k in range(6, 10):
        loads[k].wait()

    arrive(sq, col_peers, sq_recv, sq_send)
    sums = total(sq, n_col)
    square_up = mean_up * (jnp.sum(sums[:, :128], axis=1, keepdims=True) * (1.0 / (n_rows * full_up)))
    square_at = mean_at * (jnp.sum(sums[:, 128:], axis=1, keepdims=True) * (1.0 / (n_rows * full_at)))
    clip_up = 1.0 / jnp.maximum(1.0, jnp.sqrt(square_up))
    clip_at = 1.0 / jnp.maximum(1.0, jnp.sqrt(square_at))
    cols_up = root_cols[:, :cu] * ((1.0 - BETA) * clip_up * jnp.sqrt(mean_up))
    cols_at = root_cols[:, cu:] * ((1.0 - BETA) * clip_at * jnp.sqrt(mean_at))

    off_up = pl.multiple_of(col * cu, cu)
    off_at = pl.multiple_of(col * ca, ca)

    def advance(up, r0, n):
        vg, vm, vp, new_p, new_m, copy_ref, root, cols, off, width = (
            (vg_up, vm_up, vp_up, np_up, nm_up, cp_up, root_up, cols_up, off_up, cu)
            if up
            else (vg_at, vm_at, vp_at, np_at, nm_at, cp_at, root_at, cols_at, off_at, ca)
        )
        for s in range(r0, r0 + n, 16):
            here = slice(s, s + 16)
            wide = vg[here, :].astype(F32)
            mom = (BETA * vm[here, :].astype(F32) + wide * root[here, :] * cols).astype(BF16)
            new_m[here, :] = mom
            param = vp[here, :] - RATE * mom.astype(F32)
            new_p[here, :] = param
            copy_ref[here, pl.ds(off, width)] = param.astype(BF16)

    n_u, n_a = 8, 2
    hu, ha = rows // n_u, rows // n_a
    pieces = [(True, k * hu, hu) for k in range(n_u)] + [(False, k * ha, ha) for k in range(n_a)]
    rightward = [0, 1, 2, 3, 8]
    leftward = [4, 5, 6, 7, 9]

    right = (row, lax.rem(x + 1, nx) * 2 + core)
    left = (row, lax.rem(x + nx - 1, nx) * 2 + core)
    across = lax.rem(x + 2, nx) * 2 + core
    sibling = (row, x * 2 + 1 - core)
    sib_col = x * 2 + 1 - core

    def view(piece, owner):
        up, r0, n = pieces[piece]
        if up:
            return cp_up.at[pl.ds(r0, n), pl.ds(pl.multiple_of(owner * cu, cu), cu)]
        return cp_at.at[pl.ds(r0, n), pl.ds(pl.multiple_of(owner * ca, ca), ca)]

    def block(up, owner):
        if up:
            return cp_up.at[:, pl.ds(pl.multiple_of(owner * cu, cu), cu)]
        return cp_at.at[:, pl.ds(pl.multiple_of(owner * ca, ca), ca)]

    def push(piece, owner, dev, send, recv):
        pltpu.make_async_remote_copy(
            src_ref=view(piece, owner),
            dst_ref=view(piece, owner),
            send_sem=send,
            recv_sem=recv,
            device_id=dev,
            device_id_type=MESH,
        ).start()

    def await_recv(ref, recv):
        pltpu.make_async_remote_copy(
            src_ref=ref, dst_ref=ref, send_sem=sib_send.at[0, 0], recv_sem=recv,
            device_id=sibling, device_id_type=MESH,
        ).wait_recv()

    def await_send(ref, send):
        pltpu.make_async_remote_copy(
            src_ref=ref, dst_ref=ref, send_sem=send, recv_sem=far_recv.at[0],
            device_id=sibling, device_id_type=MESH,
        ).wait_send()

    kind = lambda piece: 0 if pieces[piece][0] else 1
    order = [p for pair in zip(rightward, leftward) for p in pair]
    for p in order:
        advance(*pieces[p])
        first, second = (right, left) if p in rightward else (left, right)
        to_first, to_second = (0, 1) if p in rightward else (1, 0)
        push(p, col, first, own_send.at[to_first, kind(p)], near_recv.at[to_first, p])
        push(p, col, second, own_send.at[to_second, kind(p)], near_recv.at[to_second, p])
        push(p, col, sibling, sib_send.at[0, kind(p)], sib_recv.at[0, kind(p)])

    lane4 = lax.broadcasted_iota(jnp.int32, (1, 128), 1)
    four = jnp.where(
        lane4 == 0, mean_up, jnp.where(lane4 == 1, mean_at, jnp.where(lane4 == 2, square_up, square_at))
    )
    logs[...] = jnp.log(four)

    left_col, right_col = left[1], right[1]
    for a, b in zip(rightward, leftward):
        await_recv(view(a, left_col), near_recv.at[0, a])
        push(a, left_col, right, far_send.at[0, kind(a)], far_recv.at[a])
        push(a, left_col, sibling, sib_send.at[1, kind(a)], sib_recv.at[1, kind(a)])
        await_recv(view(b, right_col), near_recv.at[1, b])
        push(b, right_col, left, far_send.at[1, kind(b)], far_recv.at[b])
        push(b, right_col, sibling, sib_send.at[2, kind(b)], sib_recv.at[2, kind(b)])
    for a, b in zip(rightward, leftward):
        await_recv(view(b, left_col), near_recv.at[0, b])
        push(b, left_col, sibling, sib_send.at[1, kind(b)], sib_recv.at[1, kind(b)])
        await_recv(view(a, right_col), near_recv.at[1, a])
        push(a, right_col, sibling, sib_send.at[2, kind(a)], sib_recv.at[2, kind(a)])
        await_recv(view(a, across), far_recv.at[a])
        push(a, across, sibling, sib_send.at[3, kind(a)], sib_recv.at[3, kind(a)])
        await_recv(view(b, across), far_recv.at[b])
        push(b, across, sibling, sib_send.at[3, kind(b)], sib_recv.at[3, kind(b)])

    other = lambda c: c + 1 - 2 * core
    owners = [col, left_col, right_col, across]
    for k, owner in enumerate(owners):
        for t, up in enumerate((True, False)):
            await_recv(block(up, other(owner)), sib_recv.at[k, t])
            await_send(block(up, owner), sib_send.at[k, t])
    for side in range(2):
        for t, up in enumerate((True, False)):
            await_send(block(up, col), own_send.at[side, t])
            ref = cp_up if up else cp_at
            w = cu if up else ca
            await_send(
                ref.at[pl.ds(0, rows // 2), pl.ds(pl.multiple_of(col * w, w), w)],
                far_send.at[side, t],
            )
    for copy in sent:
        copy.wait_send()


def on_device(
    dims, p_up, g_up, m_up, r_up, c_up, p_at, g_at, m_at, r_at, c_at
):
    ny, nz, nx = dims
    n_col = 2 * nx
    rows, cu = g_up.shape
    ca = g_at.shape[1]
    cw = cu + ca
    dma = pltpu.SemaphoreType.DMA
    vm = pltpu.VMEM
    scratch = [
        vm((rows, cu), BF16), vm((rows, ca), BF16),
        vm((rows, cu), BF16), vm((rows, ca), BF16),
        vm((rows, cu), F32), vm((rows, ca), F32),
        vm((1, 2 * rows), F32), vm((1, cw), F32),
        vm((2 * rows, 128), F32),
        vm((n_col, 1, 2 * rows), F32),
        vm((ny, 1, cw), F32), vm((nz, 1, cw), F32),
        vm((ny, 1, cw + 2 * rows), F32), vm((nz, 1, cw + 2 * rows), F32),
        vm((n_col, 1, 256), F32),
        dma((10,)),
        dma((n_col - 1,)), dma((n_col,)),
        dma((max(ny - 1, 1),)), dma((ny,)),
        dma((max(nz - 1, 1),)), dma((nz,)),
        dma((max(ny - 1, 1),)), dma((ny,)),
        dma((max(nz - 1, 1),)), dma((nz,)),
        dma((n_col - 1,)), dma((n_col,)),
        dma((2, 2)), dma((2, 10)), dma((2, 2)), dma((10,)), dma((4, 2)), dma((4, 2)),
    ]
    out_shape = [
        vm((rows, cu), F32), vm((rows, cu), BF16), vm((1, rows), F32), vm((1, cu), F32),
        vm((rows, cu * n_col), BF16),
        vm((rows, ca), F32), vm((rows, ca), BF16), vm((1, rows), F32), vm((1, ca), F32),
        vm((rows, ca * n_col), BF16),
        vm((1, 128), F32),
    ]
    out_shape = [jax.ShapeDtypeStruct(o.shape, o.dtype) for o in out_shape]
    anywhere = pl.BlockSpec(memory_space=pltpu.HBM)
    inside = pl.BlockSpec(memory_space=pltpu.VMEM)
    (np_up, nm_up, nr_up, nc_up, cp_up, np_at, nm_at, nr_at, nc_at, cp_at, logs) = pl.pallas_call(
        functools.partial(body, dims),
        out_shape=out_shape,
        in_specs=[anywhere] * 10,
        out_specs=[inside] * 11,
        scratch_shapes=scratch,
        compiler_params=pltpu.CompilerParams(
            collective_id=0, has_side_effects=True, vmem_limit_bytes=40 * 1024 * 1024
        ),
        cost_estimate=pl.CostEstimate(
            flops=20 * rows * cw, bytes_accessed=10 * rows * cw, transcendentals=0
        ),
    )(
        *[
            pltpu.with_memory_space_constraint(a, pltpu.HBM)
            for a in (
                p_up, g_up, m_up, r_up.reshape(1, rows), c_up.reshape(1, cu),
                p_at, g_at, m_at, r_at.reshape(1, rows), c_at.reshape(1, ca),
            )
        ]
    )
    return (
        np_up, nm_up, nr_up.reshape(rows), nc_up.reshape(cu), cp_up,
        np_at, nm_at, nr_at.reshape(rows), nc_at.reshape(ca), cp_at,
        logs[0, :4],
    )


def solution(mesh, dims=(4, 8, 4)):
    block = P("row", "col")
    in_specs = (block, block, block, P("row"), P("col")) * 2
    out_specs = (block, block, P("row"), P("col"), P("row", None)) * 2 + (P(),)
    return jax.shard_map(
        functools.partial(on_device, dims),
        mesh=mesh,
        in_specs=in_specs,
        out_specs=out_specs,
        check_vma=False,
    )
```

time: 324 us -> 61.8 us (0.19)
  blocking collectives: 233 us -> 0 us
  waiting for transfers between devices: 53.9 us -> 0 us
  Pallas kernels: 0 us -> 52.2 us
  between operations: 17 us -> 0.66 us
  other arithmetic: 14.6 us -> 0 us
    psum x3 -> x0, blocking collectives: 233 us -> none  [the longest x1 117 us: on_device(): sums = lax.psum((jnp.sum(new_rows_up), jnp.sum(new_rows_attn)), 'row')]
    all_gather x2 -> x0, waiting for transfers between devices: 53.9 us -> none  [the longest x1 37 us: on_device(): lax.all_gather(lowered_up, 'col', axis=1, tiled=True)]
    pallas_call x0 -> x1, Pallas kernels: none -> 52.2 us  [on_device(): pl.pallas_call(functools.partial(body, dims), out_shape=out_shape, in_spe...]
    reduce_sum x5 -> x0, other arithmetic: 7.26 us -> none  [the longest x2 3.66 us: normed(): return jnp.sum(update * update)]
    convert_element_type x2 -> x0, other arithmetic: 5.32 us -> none  [advance(): return (new_param, new_mom, new_param.astype(jnp.bfloat16))]
    unnamed x12 -> x10, local copies, waits for them, and re-layouts: 5.65 us -> 8.3 us
  transfers between devices with their start and end apart: 2 -> 0, of which waited for: 2 -> 0; matrix products, arithmetic and copies ran while one was open for 1% -> 0% of each run, Pallas kernels for 0% -> 0%
where the time goes in v1:
time: 61.8 us; the launch traced here: 61.7 us
  Pallas kernels  52.2 us (84%)
  local copies, waits for them, and re-layouts  8.81 us (14%)
  between operations  0.66 us (1%)
    pallas_call x1, Pallas kernels, on_device(): pl.pallas_call(functools.partial(body, dims), out_shape=out_shape, in_spe...  52.2 us
    unnamed x10, local copies, waits for them, and re-layouts  8.3 us

profile of v1, /device:TPU:1, one launch (start us, length us, event | category | flops | bytes accessed | tf_op | source)
XLA Modules:
  0.0 61.7 jit_solution(17261400228530029741)
XLA Ops:
  0.6 52.2 %shard_map.185 = (f32[128,2048]{1,0:T(8,128)S(1)}, bf16[128,2048]{1,0:T(8,128)(2,1)S(1)}, f32[1,128]{1,0:T(1,128)S(1)}, f32[1,2048]{1,0:T(1,128)S(1)}, bf16[128,...) custom-call(f32[128,2048]{1,0:T(8,128)} %p_up.1, ...), custom_call_target="tpu_custom_call" | custom-call | flops 6553600 | bytes 3276800 | tf_op jit(solution)/shard_map/pallas_call | solution.py:368
  52.8 0.5 slice_bitcast_fusion
  53.4 1.0 %copy.31 = f32[128,2048]{1,0:T(8,128)} copy(f32[128,2048]{1,0:T(8,128)S(1)} %get-tuple-element.44) | data formatting | bytes 2097152
  54.3 0.8 %copy.32 = bf16[128,2048]{1,0:T(8,128)(2,1)} copy(bf16[128,2048]{1,0:T(8,128)(2,1)S(1)} %get-tuple-element.45) | data formatting | bytes 1048576
  55.1 0.5 copy.33
  55.6 0.6 copy.34
  56.2 2.0 %copy.35 = bf16[128,16384]{1,0:T(8,128)(2,1)} copy(bf16[128,16384]{1,0:T(8,128)(2,1)S(1)} %get-tuple-element.48) | data formatting | bytes 8388608
  58.2 0.7 %copy.36 = f32[128,512]{1,0:T(8,128)} copy(f32[128,512]{1,0:T(8,128)S(1)} %get-tuple-element.49) | data formatting | bytes 524288
  58.9 0.7 %copy.37 = bf16[128,512]{1,0:T(8,128)(2,1)} copy(bf16[128,512]{1,0:T(8,128)(2,1)S(1)} %get-tuple-element.50) | data formatting | bytes 262144
  59.6 0.5 copy.38
  60.1 0.6 copy.39
  60.7 1.0 %copy.40 = bf16[128,4096]{1,0:T(8,128)(2,1)} copy(bf16[128,4096]{1,0:T(8,128)(2,1)S(1)} %get-tuple-element.53) | data formatting | bytes 2097152

commit v2 on v1

--- a/solution.py
+++ b/solution.py
@@ -14,6 +14,8 @@
 
 MESH = pl.DeviceIdType.MESH
 F32 = jnp.float32
+N_UP, N_AT = 8, 2
+EARLY = 4
 BF16 = jnp.bfloat16
 
 
@@ -22,10 +24,12 @@
     p_up, g_up, m_up, r_up, c_up, p_at, g_at, m_at, r_at, c_at,
     np_up, nm_up, nr_up, nc_up, cp_up, np_at, nm_at, nr_at, nc_at, cp_at, logs,
     vg_up, vg_at, vm_up, vm_at, vp_up, vp_at, vr, vc,
+    part_a, far_a, far_g, col_box,
     lane_part, rs, cs_y, cs_z, tt_y, tt_z, sq, in_sem,
     rs_send, rs_recv, cy_send, cy_recv, cz_send, cz_recv,
     ty_send, ty_recv, tz_send, tz_recv, sq_send, sq_recv,
     own_send, near_recv, far_send, far_recv, sib_send, sib_recv,
+    early_send, early_recv, relay_send, relay_recv, box_send, box_recv,
 ):
     ny, nz, nx = dims
     n_col = 2 * nx
@@ -144,6 +148,43 @@
     sent += spread(rs, col, col_devs, col_peers, rs_send, rs_recv)
     sent += spread(cs_y, y, y_devs, y_peers, cy_send, cy_recv)
 
+    hu, ha = rows // N_UP, rows // N_AT
+    early_rows = EARLY * hu
+    right = (row, lax.rem(x + 1, nx) * 2 + core)
+    left = (row, lax.rem(x + nx - 1, nx) * 2 + core)
+    across = lax.rem(x + 2, nx) * 2 + core
+    sibling = (row, x * 2 + 1 - core)
+    early_right = list(range(0, EARLY // 2))
+    early_left = list(range(EARLY // 2, EARLY))
+    early_order = [p for pair in zip(early_right, early_left) for p in pair]
+    for k in range(6, 8):
+        loads[k].wait()
+    for p in range(EARLY):
+        for r0 in range(p * hu, (p + 1) * hu, 16):
+            here = slice(r0, r0 + 16)
+            part_a[here, :] = (vp_up[here, :] - (RATE * BETA) * vm_up[here, :].astype(F32)).astype(BF16)
+
+    def early_copy(p, which, src, dst, dev, send, recv):
+        return pltpu.make_async_remote_copy(
+            src_ref=src.at[pl.ds(p * hu, hu), :],
+            dst_ref=dst.at[pl.ds(p * hu, hu), :],
+            send_sem=send,
+            recv_sem=recv,
+            device_id=dev,
+            device_id_type=MESH,
+        )
+
+    for p in early_order:
+        sides = (0, 1) if p in early_right else (1, 0)
+        for side in sides:
+            for which, (src, box) in enumerate(((part_a, far_a), (vg_up, far_g))):
+                copy = early_copy(
+                    p, which, src, box.at[side], (right, left)[side],
+                    early_send.at[side, p, which], early_recv.at[side, p, which],
+                )
+                copy.start()
+                sent.append(copy)
+
     for k in range(2, 6):
         loads[k].wait()
     arrive(rs, col_peers, rs_recv, rs_send)
@@ -187,6 +228,17 @@
     root_cols = lax.rsqrt(new_cols)
     root_up = lax.rsqrt(nr_col_up)
     root_at = lax.rsqrt(nr_col_at)
+    x_devs = [(row, lax.rem(x + k, nx) * 2 + core) for k in range(1, nx)]
+    if EARLY:
+        col_box[0] = root_cols[:, :cu]
+        for k in range(1, nx):
+            copy = pltpu.make_async_remote_copy(
+                src_ref=col_box.at[0], dst_ref=col_box.at[nx - k],
+                send_sem=box_send.at[k], recv_sem=box_recv.at[nx - k],
+                device_id=x_devs[k - 1], device_id_type=MESH,
+            )
+            copy.start()
+            sent.append(copy)
 
     arrive(tt_z, z_peers, tz_recv, tz_send)
     tt = total(tt_z, nz)
@@ -198,8 +250,21 @@
     sent += spread(sq, col, col_devs, col_peers, sq_send, sq_recv)
     mean_up = jnp.sum(tt[:, cw : cw + rows], axis=1, keepdims=True) * (1.0 / n_rows)
     mean_at = jnp.sum(tt[:, cw + rows :], axis=1, keepdims=True) * (1.0 / n_rows)
-    for k in range(6, 10):
+    for k in range(8, 10):
         loads[k].wait()
+    for p in early_order:
+        side = 0 if p in early_right else 1
+        for which, (src, box) in enumerate(((part_a, far_a), (vg_up, far_g))):
+            early_copy(
+                p, which, src, box.at[side], (right, left)[side],
+                early_send.at[side, p, which], early_recv.at[side, p, which],
+            ).wait_recv()
+            copy = early_copy(
+                p, which, box.at[side], box.at[2], (right, left)[side],
+                relay_send.at[p, which], relay_recv.at[p, which],
+            )
+            copy.start()
+            sent.append(copy)
 
     arrive(sq, col_peers, sq_recv, sq_send)
     sums = total(sq, n_col)
@@ -213,7 +278,7 @@
     off_up = pl.multiple_of(col * cu, cu)
     off_at = pl.multiple_of(col * ca, ca)
 
-    def advance(up, r0, n):
+    def advance(up, r0, n, early=False):
         vg, vm, vp, new_p, new_m, copy_ref, root, cols, off, width = (
             (vg_up, vm_up, vp_up, np_up, nm_up, cp_up, root_up, cols_up, off_up, cu)
             if up
@@ -226,19 +291,24 @@
             new_m[here, :] = mom
             param = vp[here, :] - RATE * mom.astype(F32)
             new_p[here, :] = param
-            copy_ref[here, pl.ds(off, width)] = param.astype(BF16)
-
-    n_u, n_a = 8, 2
-    hu, ha = rows // n_u, rows // n_a
-    pieces = [(True, k * hu, hu) for k in range(n_u)] + [(False, k * ha, ha) for k in range(n_a)]
-    rightward = [0, 1, 2, 3, 8]
-    leftward = [4, 5, 6, 7, 9]
-
-    right = (row, lax.rem(x + 1, nx) * 2 + core)
-    left = (row, lax.rem(x + nx - 1, nx) * 2 + core)
-    across = lax.rem(x + 2, nx) * 2 + core
-    sibling = (row, x * 2 + 1 - core)
-    sib_col = x * 2 + 1 - core
+            if not early:
+                copy_ref[here, pl.ds(off, width)] = param.astype(BF16)
+
+    scale_up = RATE * (1.0 - BETA) * clip_up * jnp.sqrt(mean_up)
+
+    def finish(a_ref, g_ref, roots, owner, p):
+        scaled = roots * scale_up
+        for r0 in range(p * hu, (p + 1) * hu, 16):
+            here = slice(r0, r0 + 16)
+            step = g_ref[here, :].astype(F32) * root_up[here, :] * scaled
+            cp_up[here, pl.ds(pl.multiple_of(owner * cu, cu), cu)] = (
+                a_ref[here, :].astype(F32) - step
+            ).astype(BF16)
+
+    pieces = [(True, k * hu, hu) for k in range(N_UP)] + [(False, k * ha, ha) for k in range(N_AT)]
+    mid = (EARLY + N_UP) // 2
+    rightward = list(range(EARLY, mid)) + [N_UP]
+    leftward = list(range(mid, N_UP)) + [N_UP + 1]
 
     def view(piece, owner):
         up, r0, n = pieces[piece]
@@ -283,13 +353,45 @@
         push(p, col, second, own_send.at[to_second, kind(p)], near_recv.at[to_second, p])
         push(p, col, sibling, sib_send.at[0, kind(p)], sib_recv.at[0, kind(p)])
 
+    for p in range(EARLY):
+        advance(*pieces[p], early=True)
+        finish(part_a, vg_up, col_box[0], col, p)
+        push(p, col, sibling, sib_send.at[0, 0], sib_recv.at[0, 0])
+
     lane4 = lax.broadcasted_iota(jnp.int32, (1, 128), 1)
     four = jnp.where(
         lane4 == 0, mean_up, jnp.where(lane4 == 1, mean_at, jnp.where(lane4 == 2, square_up, square_at))
     )
-    logs[...] = jnp.log(four)
+    logs[...] = jnp.log(four)[:, :4]
 
     left_col, right_col = left[1], right[1]
+    if EARLY:
+        for k in range(1, nx):
+            pltpu.make_async_remote_copy(
+                src_ref=col_box.at[0], dst_ref=col_box.at[k],
+                send_sem=box_send.at[k], recv_sem=box_recv.at[k],
+                device_id=x_devs[0], device_id_type=MESH,
+            ).wait_recv()
+
+    def finish_box(side, owner, box, p):
+        if box == 2:
+            for which, (src, arrived) in enumerate(((part_a, far_a), (vg_up, far_g))):
+                early_copy(
+                    p, which, src, arrived.at[2], right, relay_send.at[p, which], relay_recv.at[p, which]
+                ).wait_recv()
+        elif p not in (early_right, early_left)[box]:
+            for which, (src, arrived) in enumerate(((part_a, far_a), (vg_up, far_g))):
+                early_copy(
+                    p, which, src, arrived.at[box], right,
+                    early_send.at[box, p, which], early_recv.at[box, p, which],
+                ).wait_recv()
+        finish(far_a.at[box], far_g.at[box], col_box[side], owner, p)
+        k = {0: 1, 1: 2, 2: 3}[box]
+        push(p, owner, sibling, sib_send.at[k, 0], sib_recv.at[k, 0])
+
+    for p in range(EARLY):
+        finish_box(3, left_col, 0, p)
+        finish_box(1, right_col, 1, p)
     for a, b in zip(rightward, leftward):
         await_recv(view(a, left_col), near_recv.at[0, a])
         push(a, left_col, right, far_send.at[0, kind(a)], far_recv.at[a])
@@ -297,6 +399,8 @@
         await_recv(view(b, right_col), near_recv.at[1, b])
         push(b, right_col, left, far_send.at[1, kind(b)], far_recv.at[b])
         push(b, right_col, sibling, sib_send.at[2, kind(b)], sib_recv.at[2, kind(b)])
+    for p in early_order:
+        finish_box(2, across, 2, p)
     for a, b in zip(rightward, leftward):
         await_recv(view(b, left_col), near_recv.at[0, b])
         push(b, left_col, sibling, sib_send.at[1, kind(b)], sib_recv.at[1, kind(b)])
@@ -313,17 +417,27 @@
         for t, up in enumerate((True, False)):
             await_recv(block(up, other(owner)), sib_recv.at[k, t])
             await_send(block(up, owner), sib_send.at[k, t])
+    late = rows - early_rows
     for side in range(2):
-        for t, up in enumerate((True, False)):
-            await_send(block(up, col), own_send.at[side, t])
-            ref = cp_up if up else cp_at
-            w = cu if up else ca
-            await_send(
-                ref.at[pl.ds(0, rows // 2), pl.ds(pl.multiple_of(col * w, w), w)],
-                far_send.at[side, t],
-            )
+        for t, (ref, n, w) in enumerate(((cp_up, late, cu), (cp_at, rows, ca))):
+            here = pl.ds(pl.multiple_of(col * w, w), w)
+            await_send(ref.at[pl.ds(0, n), here], own_send.at[side, t])
+            await_send(ref.at[pl.ds(0, n // 2), here], far_send.at[side, t])
     for copy in sent:
         copy.wait_send()
+
+
+def write_out(*refs):
+    n = (len(refs) - 1) // 2
+    sems = refs[-1]
+    copies = [
+        pltpu.make_async_copy(src, dst, sems.at[i])
+        for i, (src, dst) in enumerate(zip(refs[:n], refs[n : 2 * n]))
+    ]
+    for copy in copies:
+        copy.start()
+    for copy in copies:
+        copy.wait()
 
 
 def on_device(
@@ -334,6 +448,8 @@
     rows, cu = g_up.shape
     ca = g_at.shape[1]
     cw = cu + ca
+    n_early = max(EARLY, 1)
+    early = n_early * (rows // N_UP)
     dma = pltpu.SemaphoreType.DMA
     vm = pltpu.VMEM
     scratch = [
@@ -341,6 +457,7 @@
         vm((rows, cu), BF16), vm((rows, ca), BF16),
         vm((rows, cu), F32), vm((rows, ca), F32),
         vm((1, 2 * rows), F32), vm((1, cw), F32),
+        vm((early, cu), BF16), vm((3, early, cu), BF16), vm((3, early, cu), BF16), vm((nx, 1, cu), F32),
         vm((2 * rows, 128), F32),
         vm((n_col, 1, 2 * rows), F32),
         vm((ny, 1, cw), F32), vm((nz, 1, cw), F32),
@@ -354,18 +471,19 @@
         dma((max(nz - 1, 1),)), dma((nz,)),
         dma((n_col - 1,)), dma((n_col,)),
         dma((2, 2)), dma((2, 10)), dma((2, 2)), dma((10,)), dma((4, 2)), dma((4, 2)),
+        dma((2, n_early, 2)), dma((2, n_early, 2)), dma((n_early, 2)), dma((n_early, 2)),
+        dma((nx,)), dma((nx,)),
     ]
     out_shape = [
         vm((rows, cu), F32), vm((rows, cu), BF16), vm((1, rows), F32), vm((1, cu), F32),
         vm((rows, cu * n_col), BF16),
         vm((rows, ca), F32), vm((rows, ca), BF16), vm((1, rows), F32), vm((1, ca), F32),
         vm((rows, ca * n_col), BF16),
-        vm((1, 128), F32),
+        vm((1, 4), F32),
     ]
-    out_shape = [jax.ShapeDtypeStruct(o.shape, o.dtype) for o in out_shape]
     anywhere = pl.BlockSpec(memory_space=pltpu.HBM)
     inside = pl.BlockSpec(memory_space=pltpu.VMEM)
-    (np_up, nm_up, nr_up, nc_up, cp_up, np_at, nm_at, nr_at, nc_at, cp_at, logs) = pl.pallas_call(
+    results = pl.pallas_call(
         functools.partial(body, dims),
         out_shape=out_shape,
         in_specs=[anywhere] * 10,
@@ -386,10 +504,21 @@
             )
         ]
     )
+    (np_up, nm_up, nr_up, nc_up, cp_up, np_at, nm_at, nr_at, nc_at, cp_at, logs) = pl.pallas_call(
+        write_out,
+        out_shape=[pltpu.HBM(o.shape, o.dtype) for o in out_shape],
+        in_specs=[inside] * 11,
+        out_specs=[anywhere] * 11,
+        scratch_shapes=[dma((11,))],
+        compiler_params=pltpu.CompilerParams(vmem_limit_bytes=1024 * 1024),
+        cost_estimate=pl.CostEstimate(
+            flops=0, bytes_accessed=2 * rows * cw * (n_col + 3), transcendentals=0
+        ),
+    )(*[pltpu.with_memory_space_constraint(r, pltpu.VMEM) for r in results])
     return (
         np_up, nm_up, nr_up.reshape(rows), nc_up.reshape(cu), cp_up,
         np_at, nm_at, nr_at.reshape(rows), nc_at.reshape(ca), cp_at,
-        logs[0, :4],
+        logs.reshape(4),
     )
 
 

time: 61.8 us -> 48.8 us (0.79)
  local copies, waits for them, and re-layouts: 8.81 us -> 0 us
  Pallas kernels: 52.2 us -> 48.1 us
    unnamed x10 -> x0, local copies, waits for them, and re-layouts: 8.3 us -> none
    pallas_call x1, Pallas kernels: 52.2 us -> 45 us  [on_device(): pl.pallas_call(functools.partial(body, dims), out_shape=out_shape, in_spe...]
    pallas_call x0 -> x1, Pallas kernels: none -> 3.11 us  [on_device(): pl.pallas_call(write_out, out_shape=[pltpu.HBM(o.shape, o.dtype) for o in...]
where the time goes in v2:
time: 48.8 us; the launch traced here: 48.7 us
  Pallas kernels  48.1 us (99%)
  between operations  0.66 us (1%)
    pallas_call x1, Pallas kernels, on_device(): pl.pallas_call(functools.partial(body, dims), out_shape=out_shape, in_spe...  45 us
    pallas_call x1, Pallas kernels, on_device(): pl.pallas_call(write_out, out_shape=[pltpu.HBM(o.shape, o.dtype) for o in...  3.11 us

profile of v2, /device:TPU:1, one launch (start us, length us, event | category | flops | bytes accessed | tf_op | source)
XLA Modules:
  0.0 48.7 jit_solution(6143069491252997772)
XLA Ops:
  0.6 45.0 %shard_map.185 = (f32[128,2048]{1,0:T(8,128)S(1)}, bf16[128,2048]{1,0:T(8,128)(2,1)S(1)}, f32[1,128]{1,0:T(1,128)S(1)}, f32[1,2048]{1,0:T(1,128)S(1)}, bf16[128,...) custom-call(f32[128,2048]{1,0:T(8,128)} %p_up.1, ...), custom_call_target="tpu_custom_call" | custom-call | flops 6553600 | bytes 3276800 | tf_op jit(solution)/shard_map/pallas_call | solution.py:486
  45.6 3.1 %shard_map.186 = (f32[128,2048]{1,0:T(8,128)}, bf16[128,2048]{1,0:T(8,128)(2,1)}, f32[1,128]{1,0:T(1,128)}, f32[1,2048]{1,0:T(1,128)}, bf16[128,16384]{1,0:T(8,1...) custom-call(f32[128,2048]{1,0:T(8,128)S(1)} %get-tuple-element.33.re, ...), custom_call_target="tpu_custom_call" | custom-call | bytes 7208960 | tf_op jit(solution)/shard_map/pallas_call | solution.py:507

commit v3 on v2

--- a/solution.py
+++ b/solution.py
@@ -14,8 +14,8 @@
 
 MESH = pl.DeviceIdType.MESH
 F32 = jnp.float32
-N_UP, N_AT = 8, 2
-EARLY = 4
+STEP = 16
+EARLY = 80
 BF16 = jnp.bfloat16
 
 
@@ -29,7 +29,7 @@
     rs_send, rs_recv, cy_send, cy_recv, cz_send, cz_recv,
     ty_send, ty_recv, tz_send, tz_recv, sq_send, sq_recv,
     own_send, near_recv, far_send, far_recv, sib_send, sib_recv,
-    early_send, early_recv, relay_send, relay_recv, box_send, box_recv,
+    wave_send, wave_recv, box_send, box_recv, row_ready, ring_ready,
 ):
     ny, nz, nx = dims
     n_col = 2 * nx
@@ -47,15 +47,18 @@
 
     col_peers = [lax.rem(col + k, n_col) for k in range(1, n_col)]
     y_peers = [lax.rem(y + k, ny) for k in range(1, ny)]
-    z_peers = [lax.rem(z + k, nz) for k in range(1, nz)]
+    z_peers = [lax.rem(z + k, nz) for k in sorted(range(1, nz), key=lambda k: -min(k, nz - k))]
 
     barrier = pltpu.get_barrier_semaphore()
-    for c in col_peers:
-        pl.semaphore_signal(barrier, inc=1, device_id=(row, c), device_id_type=MESH)
-    for q in y_peers:
-        pl.semaphore_signal(barrier, inc=1, device_id=(q * nz + z, col), device_id_type=MESH)
-    for q in z_peers:
-        pl.semaphore_signal(barrier, inc=1, device_id=(y * nz + q, col), device_id_type=MESH)
+    sib = (row, x * 2 + 1 - core)
+    for k in range(1, nx):
+        there = (row, lax.rem(x + k, nx) * 2)
+        pl.semaphore_signal(barrier, inc=1, device_id=there, device_id_type=MESH)
+    pl.when(core == 1)(
+        lambda: pl.semaphore_signal(barrier, inc=1, device_id=sib, device_id_type=MESH)
+    )
+    for q in [y * nz + q for q in z_peers] + [q * nz + z for q in y_peers]:
+        pl.semaphore_signal(barrier, inc=1, device_id=(q, x * 2 + 1), device_id_type=MESH)
 
     loads = [
         pltpu.make_async_copy(src, dst, in_sem.at[i])
@@ -110,7 +113,20 @@
     sums = jnp.sum(lane_part[...], axis=1, keepdims=True)
     rs[col] = jnp.concatenate([to_lanes(sums[:rows]), to_lanes(sums[rows:])], axis=1)
 
-    pl.semaphore_wait(barrier, (n_col - 1) + (ny - 1) + (nz - 1))
+    for k in range(6, 8):
+        loads[k].wait()
+    for r0 in range(0, EARLY, 16):
+        here = slice(r0, r0 + 16)
+        part_a[here, :] = (vp_up[here, :] - (RATE * BETA) * vm_up[here, :].astype(F32)).astype(BF16)
+
+    @pl.when(core == 0)
+    def _():
+        pl.semaphore_wait(barrier, n_col - 1)
+        pl.semaphore_signal(row_ready, inc=1, device_id=sib, device_id_type=MESH)
+
+    @pl.when(core == 1)
+    def _():
+        pl.semaphore_wait(row_ready, 1)
 
     def spread(buf, slot, targets, peers, send, recv):
         out = []
@@ -146,44 +162,54 @@
     z_devs = [(y * nz + q, col) for q in z_peers]
     sent = []
     sent += spread(rs, col, col_devs, col_peers, rs_send, rs_recv)
-    sent += spread(cs_y, y, y_devs, y_peers, cy_send, cy_recv)
-
-    hu, ha = rows // N_UP, rows // N_AT
-    early_rows = EARLY * hu
+
     right = (row, lax.rem(x + 1, nx) * 2 + core)
     left = (row, lax.rem(x + nx - 1, nx) * 2 + core)
     across = lax.rem(x + 2, nx) * 2 + core
     sibling = (row, x * 2 + 1 - core)
-    early_right = list(range(0, EARLY // 2))
-    early_left = list(range(EARLY // 2, EARLY))
-    early_order = [p for pair in zip(early_right, early_left) for p in pair]
-    for k in range(6, 8):
-        loads[k].wait()
-    for p in range(EARLY):
-        for r0 in range(p * hu, (p + 1) * hu, 16):
-            here = slice(r0, r0 + 16)
-            part_a[here, :] = (vp_up[here, :] - (RATE * BETA) * vm_up[here, :].astype(F32)).astype(BF16)
-
-    def early_copy(p, which, src, dst, dev, send, recv):
+    ways = (right, left)
+    half = cu // 2
+
+    def early_copy(wave, way, which, part, box):
+        src = ((part_a, vg_up) if wave != 1 else (far_a.at[way], far_g.at[way]))[which]
+        dst = (far_a, far_g)[which].at[box]
+        rows_, cols_ = pl.ds(0, EARLY), pl.ds(part * half, half)
         return pltpu.make_async_remote_copy(
-            src_ref=src.at[pl.ds(p * hu, hu), :],
-            dst_ref=dst.at[pl.ds(p * hu, hu), :],
-            send_sem=send,
-            recv_sem=recv,
-            device_id=dev,
+            src_ref=src.at[rows_, cols_],
+            dst_ref=dst.at[rows_, cols_],
+            send_sem=wave_send.at[wave, way, which],
+            recv_sem=wave_recv.at[wave, way, which],
+            device_id=ways[way],
             device_id_type=MESH,
         )
 
-    for p in early_order:
-        sides = (0, 1) if p in early_right else (1, 0)
-        for side in sides:
-            for which, (src, box) in enumerate(((part_a, far_a), (vg_up, far_g))):
-                copy = early_copy(
-                    p, which, src, box.at[side], (right, left)[side],
-                    early_send.at[side, p, which], early_recv.at[side, p, which],
-                )
+    def early_args(wave, way):
+        return (way, (way, 2, way)[wave]) if wave < 2 else (1 - way, way)
+
+    def start_wave(wave, parts=(0, 1)):
+        for way in range(2):
+            for which in parts:
+                copy = early_copy(wave, way, which, *early_args(wave, way))
                 copy.start()
                 sent.append(copy)
+
+    def await_wave(wave, way, parts=(0, 1)):
+        for which in parts:
+            early_copy(wave, way, which, *early_args(wave, way)).wait_recv()
+
+    start_wave(0)
+    start_wave(2)
+
+    @pl.when(core == 1)
+    def _():
+        pl.semaphore_wait(barrier, 2 * ((ny - 1) + (nz - 1)))
+        pl.semaphore_signal(ring_ready, inc=1, device_id=sib, device_id_type=MESH)
+
+    @pl.when(core == 0)
+    def _():
+        pl.semaphore_wait(ring_ready, 1)
+
+    sent += spread(cs_y, y, y_devs, y_peers, cy_send, cy_recv)
 
     for k in range(2, 6):
         loads[k].wait()
@@ -220,6 +246,7 @@
     tt_z[z] = total(tt_y, ny)
     sent += spread(tt_z, z, z_devs, z_peers, tz_send, tz_recv)
 
+
     arrive(cs_z, z_peers, cz_recv, cz_send)
     new_cols = DECAY * vc[...] + (1.0 - DECAY) * (total(cs_z, nz) * (1.0 / n_rows))
     nc_up[...] = new_cols[:, :cu]
@@ -229,7 +256,7 @@
     root_up = lax.rsqrt(nr_col_up)
     root_at = lax.rsqrt(nr_col_at)
     x_devs = [(row, lax.rem(x + k, nx) * 2 + core) for k in range(1, nx)]
-    if EARLY:
+    if True:
         col_box[0] = root_cols[:, :cu]
         for k in range(1, nx):
             copy = pltpu.make_async_remote_copy(
@@ -240,6 +267,9 @@
             copy.start()
             sent.append(copy)
 
+    for way in range(2):
+        await_wave(0, way, (0,))
+    start_wave(1, (0,))
     arrive(tt_z, z_peers, tz_recv, tz_send)
     tt = total(tt_z, nz)
     terms = tt[:, :cw] * inv_cols
@@ -252,20 +282,9 @@
     mean_at = jnp.sum(tt[:, cw + rows :], axis=1, keepdims=True) * (1.0 / n_rows)
     for k in range(8, 10):
         loads[k].wait()
-    for p in early_order:
-        side = 0 if p in early_right else 1
-        for which, (src, box) in enumerate(((part_a, far_a), (vg_up, far_g))):
-            early_copy(
-                p, which, src, box.at[side], (right, left)[side],
-                early_send.at[side, p, which], early_recv.at[side, p, which],
-            ).wait_recv()
-            copy = early_copy(
-                p, which, box.at[side], box.at[2], (right, left)[side],
-                relay_send.at[p, which], relay_recv.at[p, which],
-            )
-            copy.start()
-            sent.append(copy)
-
+    for way in range(2):
+        await_wave(0, way, (1,))
+    start_wave(1, (1,))
     arrive(sq, col_peers, sq_recv, sq_send)
     sums = total(sq, n_col)
     square_up = mean_up * (jnp.sum(sums[:, :128], axis=1, keepdims=True) * (1.0 / (n_rows * full_up)))
@@ -296,25 +315,32 @@
 
     scale_up = RATE * (1.0 - BETA) * clip_up * jnp.sqrt(mean_up)
 
-    def finish(a_ref, g_ref, roots, owner, p):
+    def finish(a_ref, g_ref, roots, owner):
         scaled = roots * scale_up
-        for r0 in range(p * hu, (p + 1) * hu, 16):
+        for r0 in range(0, EARLY, 16):
             here = slice(r0, r0 + 16)
-            step = g_ref[here, :].astype(F32) * root_up[here, :] * scaled
+            move = g_ref[here, :].astype(F32) * root_up[here, :] * scaled
             cp_up[here, pl.ds(pl.multiple_of(owner * cu, cu), cu)] = (
-                a_ref[here, :].astype(F32) - step
+                a_ref[here, :].astype(F32) - move
             ).astype(BF16)
 
-    pieces = [(True, k * hu, hu) for k in range(N_UP)] + [(False, k * ha, ha) for k in range(N_AT)]
-    mid = (EARLY + N_UP) // 2
-    rightward = list(range(EARLY, mid)) + [N_UP]
-    leftward = list(range(mid, N_UP)) + [N_UP + 1]
-
-    def view(piece, owner):
-        up, r0, n = pieces[piece]
-        if up:
-            return cp_up.at[pl.ds(r0, n), pl.ds(pl.multiple_of(owner * cu, cu), cu)]
-        return cp_at.at[pl.ds(r0, n), pl.ds(pl.multiple_of(owner * ca, ca), ca)]
+    quarter = rows // 4
+    units = [[], []]
+    chunks = []
+    for r0 in range(EARLY, rows, STEP):
+        chunks.append([(True, r0, STEP)])
+        for way in range(2):
+            units[way].append((True, r0, STEP, way * half, half))
+    for k in range(2):
+        chunks.append([(False, (2 * way + k) * quarter, quarter) for way in range(2)])
+        for way in range(2):
+            units[way].append((False, (2 * way + k) * quarter, quarter, 0, ca))
+    n_late = len(chunks)
+
+    def view(unit, owner):
+        up, r0, n, c0, w = unit
+        ref, width = (cp_up, cu) if up else (cp_at, ca)
+        return ref.at[pl.ds(r0, n), pl.ds(pl.multiple_of(owner * width + c0, w), w)]
 
     def block(up, owner):
         if up:
@@ -339,24 +365,29 @@
 
     def await_send(ref, send):
         pltpu.make_async_remote_copy(
-            src_ref=ref, dst_ref=ref, send_sem=send, recv_sem=far_recv.at[0],
+            src_ref=ref, dst_ref=ref, send_sem=send, recv_sem=far_recv.at[0, 0],
             device_id=sibling, device_id_type=MESH,
         ).wait_send()
 
-    kind = lambda piece: 0 if pieces[piece][0] else 1
-    order = [p for pair in zip(rightward, leftward) for p in pair]
-    for p in order:
-        advance(*pieces[p])
-        first, second = (right, left) if p in rightward else (left, right)
-        to_first, to_second = (0, 1) if p in rightward else (1, 0)
-        push(p, col, first, own_send.at[to_first, kind(p)], near_recv.at[to_first, p])
-        push(p, col, second, own_send.at[to_second, kind(p)], near_recv.at[to_second, p])
-        push(p, col, sibling, sib_send.at[0, kind(p)], sib_recv.at[0, kind(p)])
-
-    for p in range(EARLY):
-        advance(*pieces[p], early=True)
-        finish(part_a, vg_up, col_box[0], col, p)
-        push(p, col, sibling, sib_send.at[0, 0], sib_recv.at[0, 0])
+    kind = lambda unit: 0 if unit[0] else 1
+
+    def to_sibling(unit, owner, k):
+        push(unit, owner, sibling, sib_send.at[k, kind(unit)], sib_recv.at[k, kind(unit)])
+
+    def near(way, part, i):
+        unit = units[part][i]
+        push(unit, col, ways[way], own_send.at[way, kind(unit)], near_recv.at[way, part, i])
+
+    for i in range(n_late):
+        for up, r0, n in chunks[i]:
+            advance(up, r0, n)
+        near(0, 0, i)
+        near(1, 1, i)
+        for up, r0, n in chunks[i]:
+            to_sibling((up, r0, n, 0, cu if up else ca), col, 0)
+    advance(True, 0, EARLY, early=True)
+    finish(part_a, vg_up, col_box[0], col)
+    to_sibling((True, 0, EARLY, 0, cu), col, 0)
 
     lane4 = lax.broadcasted_iota(jnp.int32, (1, 128), 1)
     four = jnp.where(
@@ -373,58 +404,51 @@
                 device_id=x_devs[0], device_id_type=MESH,
             ).wait_recv()
 
-    def finish_box(side, owner, box, p):
-        if box == 2:
-            for which, (src, arrived) in enumerate(((part_a, far_a), (vg_up, far_g))):
-                early_copy(
-                    p, which, src, arrived.at[2], right, relay_send.at[p, which], relay_recv.at[p, which]
-                ).wait_recv()
-        elif p not in (early_right, early_left)[box]:
-            for which, (src, arrived) in enumerate(((part_a, far_a), (vg_up, far_g))):
-                early_copy(
-                    p, which, src, arrived.at[box], right,
-                    early_send.at[box, p, which], early_recv.at[box, p, which],
-                ).wait_recv()
-        finish(far_a.at[box], far_g.at[box], col_box[side], owner, p)
-        k = {0: 1, 1: 2, 2: 3}[box]
-        push(p, owner, sibling, sib_send.at[k, 0], sib_recv.at[k, 0])
-
-    for p in range(EARLY):
-        finish_box(3, left_col, 0, p)
-        finish_box(1, right_col, 1, p)
-    for a, b in zip(rightward, leftward):
-        await_recv(view(a, left_col), near_recv.at[0, a])
-        push(a, left_col, right, far_send.at[0, kind(a)], far_recv.at[a])
-        push(a, left_col, sibling, sib_send.at[1, kind(a)], sib_recv.at[1, kind(a)])
-        await_recv(view(b, right_col), near_recv.at[1, b])
-        push(b, right_col, left, far_send.at[1, kind(b)], far_recv.at[b])
-        push(b, right_col, sibling, sib_send.at[2, kind(b)], sib_recv.at[2, kind(b)])
-    for p in early_order:
-        finish_box(2, across, 2, p)
-    for a, b in zip(rightward, leftward):
-        await_recv(view(b, left_col), near_recv.at[0, b])
-        push(b, left_col, sibling, sib_send.at[1, kind(b)], sib_recv.at[1, kind(b)])
-        await_recv(view(a, right_col), near_recv.at[1, a])
-        push(a, right_col, sibling, sib_send.at[2, kind(a)], sib_recv.at[2, kind(a)])
-        await_recv(view(a, across), far_recv.at[a])
-        push(a, across, sibling, sib_send.at[3, kind(a)], sib_recv.at[3, kind(a)])
-        await_recv(view(b, across), far_recv.at[b])
-        push(b, across, sibling, sib_send.at[3, kind(b)], sib_recv.at[3, kind(b)])
-
+    def finish_box(box):
+        owner, column, waves = (
+            (left_col, 3, ((0, 0), (2, 0))), (right_col, 1, ((0, 1), (2, 1))), (across, 2, ((1, 0), (1, 1)))
+        )[box]
+        for wave, way in waves:
+            if wave:
+                await_wave(wave, way)
+        finish(far_a.at[box], far_g.at[box], col_box[column], owner)
+        to_sibling((True, 0, EARLY, 0, cu), owner, box + 1)
+
+    from_cols = (left_col, right_col)
+    for i in range(n_late):
+        if i < 3:
+            finish_box((2, 0, 1)[i])
+        for way in range(2):
+            unit, owner = units[way][i], from_cols[way]
+            await_recv(view(unit, owner), near_recv.at[way, way, i])
+            push(unit, owner, ways[way], far_send.at[way, kind(unit)], far_recv.at[way, i])
+            near(way, 1 - way, i)
+            to_sibling(unit, owner, way + 1)
+    for copy in sent:
+        copy.wait_send()
+    for i in range(n_late):
+        for way in range(2):
+            unit = units[way][i]
+            await_recv(view(unit, across), far_recv.at[way, i])
+            to_sibling(unit, across, 3)
+        for way in range(2):
+            unit = units[1 - way][i]
+            await_recv(view(unit, from_cols[way]), near_recv.at[way, 1 - way, i])
+            to_sibling(unit, from_cols[way], way + 1)
+
+    late = rows - EARLY
+    for side in range(2):
+        for t, (ref, n, w) in enumerate(((cp_up, late, cu), (cp_at, rows, ca))):
+            here = pl.ds(pl.multiple_of(col * w, w), w)
+            await_send(ref.at[pl.ds(0, n), here], own_send.at[side, t])
+            here = pl.ds(pl.multiple_of(col * w, w // 2), w // 2)
+            await_send(ref.at[pl.ds(0, n), here], far_send.at[side, t])
     other = lambda c: c + 1 - 2 * core
     owners = [col, left_col, right_col, across]
     for k, owner in enumerate(owners):
         for t, up in enumerate((True, False)):
+            await_send(block(up, owner), sib_send.at[k, t])
             await_recv(block(up, other(owner)), sib_recv.at[k, t])
-            await_send(block(up, owner), sib_send.at[k, t])
-    late = rows - early_rows
-    for side in range(2):
-        for t, (ref, n, w) in enumerate(((cp_up, late, cu), (cp_at, rows, ca))):
-            here = pl.ds(pl.multiple_of(col * w, w), w)
-            await_send(ref.at[pl.ds(0, n), here], own_send.at[side, t])
-            await_send(ref.at[pl.ds(0, n // 2), here], far_send.at[side, t])
-    for copy in sent:
-        copy.wait_send()
 
 
 def write_out(*refs):
@@ -448,8 +472,7 @@
     rows, cu = g_up.shape
     ca = g_at.shape[1]
     cw = cu + ca
-    n_early = max(EARLY, 1)
-    early = n_early * (rows // N_UP)
+    n_late = (rows - EARLY) // STEP + 2
     dma = pltpu.SemaphoreType.DMA
     vm = pltpu.VMEM
     scratch = [
@@ -457,7 +480,7 @@
         vm((rows, cu), BF16), vm((rows, ca), BF16),
         vm((rows, cu), F32), vm((rows, ca), F32),
         vm((1, 2 * rows), F32), vm((1, cw), F32),
-        vm((early, cu), BF16), vm((3, early, cu), BF16), vm((3, early, cu), BF16), vm((nx, 1, cu), F32),
+        vm((EARLY, cu), BF16), vm((3, EARLY, cu), BF16), vm((3, EARLY, cu), BF16), vm((nx, 1, cu), F32),
         vm((2 * rows, 128), F32),
         vm((n_col, 1, 2 * rows), F32),
         vm((ny, 1, cw), F32), vm((nz, 1, cw), F32),
@@ -470,9 +493,10 @@
         dma((max(ny - 1, 1),)), dma((ny,)),
         dma((max(nz - 1, 1),)), dma((nz,)),
         dma((n_col - 1,)), dma((n_col,)),
-        dma((2, 2)), dma((2, 10)), dma((2, 2)), dma((10,)), dma((4, 2)), dma((4, 2)),
-        dma((2, n_early, 2)), dma((2, n_early, 2)), dma((n_early, 2)), dma((n_early, 2)),
+        dma((2, 2)), dma((2, 2, n_late)), dma((2, 2)), dma((2, n_late)), dma((4, 2)), dma((4, 2)),
+        dma((3, 2, 2)), dma((3, 2, 2)),
         dma((nx,)), dma((nx,)),
+        pltpu.SemaphoreType.REGULAR, pltpu.SemaphoreType.REGULAR,
     ]
     out_shape = [
         vm((rows, cu), F32), vm((rows, cu), BF16), vm((1, rows), F32), vm((1, cu), F32),

time: 48.8 us -> 46.4 us (0.951)
  Pallas kernels: 48.1 us -> 45.6 us
    pallas_call x1, Pallas kernels: 45 us -> 42.5 us  [on_device(): pl.pallas_call(functools.partial(body, dims), out_shape=out_shape, in_spe...]
where the time goes in v3:
time: 46.4 us; the launch traced here: 46.2 us
  Pallas kernels  45.6 us (98%)
  between operations  0.66 us (1%)
    pallas_call x1, Pallas kernels, on_device(): pl.pallas_call(functools.partial(body, dims), out_shape=out_shape, in_spe...  42.5 us
    pallas_call x1, Pallas kernels, on_device(): pl.pallas_call(write_out, out_shape=[pltpu.HBM(o.shape, o.dtype) for o in...  3.11 us

profile of v3, /device:TPU:1, one launch (start us, length us, event | category | flops | bytes accessed | tf_op | source)
XLA Modules:
  0.0 46.2 jit_solution(4571745438516908698)
XLA Ops:
  0.6 42.5 %shard_map.185 = (f32[128,2048]{1,0:T(8,128)S(1)}, bf16[128,2048]{1,0:T(8,128)(2,1)S(1)}, f32[1,128]{1,0:T(1,128)S(1)}, f32[1,2048]{1,0:T(1,128)S(1)}, bf16[128,...) custom-call(f32[128,2048]{1,0:T(8,128)} %p_up.1, ...), custom_call_target="tpu_custom_call" | custom-call | flops 6553600 | bytes 3276800 | tf_op jit(solution)/shard_map/pallas_call | solution.py:510
  43.1 3.1 %shard_map.186 = (f32[128,2048]{1,0:T(8,128)}, bf16[128,2048]{1,0:T(8,128)(2,1)}, f32[1,128]{1,0:T(1,128)}, f32[1,2048]{1,0:T(1,128)}, bf16[128,16384]{1,0:T(8,1...) custom-call(f32[128,2048]{1,0:T(8,128)S(1)} %get-tuple-element.33.re, ...), custom_call_target="tpu_custom_call" | custom-call | bytes 7208960 | tf_op jit(solution)/shard_map/pallas_call | solution.py:531

commit v4 on v3

--- a/solution.py
+++ b/solution.py
@@ -14,8 +14,10 @@
 
 MESH = pl.DeviceIdType.MESH
 F32 = jnp.float32
+RELAY = 32
+AHEAD = 32
 STEP = 16
-EARLY = 80
+EARLY = 96
 BF16 = jnp.bfloat16
 
 
@@ -29,7 +31,7 @@
     rs_send, rs_recv, cy_send, cy_recv, cz_send, cz_recv,
     ty_send, ty_recv, tz_send, tz_recv, sq_send, sq_recv,
     own_send, near_recv, far_send, far_recv, sib_send, sib_recv,
-    wave_send, wave_recv, box_send, box_recv, row_ready, ring_ready,
+    wave_send, wave_recv, ahead_send, ahead_recv, relay_recv, box_send, box_recv, row_ready, ring_ready,
 ):
     ny, nz, nx = dims
     n_col = 2 * nx
@@ -113,12 +115,6 @@
     sums = jnp.sum(lane_part[...], axis=1, keepdims=True)
     rs[col] = jnp.concatenate([to_lanes(sums[:rows]), to_lanes(sums[rows:])], axis=1)
 
-    for k in range(6, 8):
-        loads[k].wait()
-    for r0 in range(0, EARLY, 16):
-        here = slice(r0, r0 + 16)
-        part_a[here, :] = (vp_up[here, :] - (RATE * BETA) * vm_up[here, :].astype(F32)).astype(BF16)
-
     @pl.when(core == 0)
     def _():
         pl.semaphore_wait(barrier, n_col - 1)
@@ -162,6 +158,12 @@
     z_devs = [(y * nz + q, col) for q in z_peers]
     sent = []
     sent += spread(rs, col, col_devs, col_peers, rs_send, rs_recv)
+    for k in range(6, 8):
+        loads[k].wait()
+    for r0 in range(0, EARLY, 16):
+        here = slice(r0, r0 + 16)
+        part_a[here, :] = (vp_up[here, :] - (RATE * BETA) * vm_up[here, :].astype(F32)).astype(BF16)
+
 
     right = (row, lax.rem(x + 1, nx) * 2 + core)
     left = (row, lax.rem(x + nx - 1, nx) * 2 + core)
@@ -170,36 +172,23 @@
     ways = (right, left)
     half = cu // 2
 
-    def early_copy(wave, way, which, part, box):
-        src = ((part_a, vg_up) if wave != 1 else (far_a.at[way], far_g.at[way]))[which]
-        dst = (far_a, far_g)[which].at[box]
-        rows_, cols_ = pl.ds(0, EARLY), pl.ds(part * half, half)
+    def early_copy(way, which):
+        src, dst = ((part_a, far_a), (vg_up.at[pl.ds(0, EARLY), :], far_g))[which]
         return pltpu.make_async_remote_copy(
-            src_ref=src.at[rows_, cols_],
-            dst_ref=dst.at[rows_, cols_],
-            send_sem=wave_send.at[wave, way, which],
-            recv_sem=wave_recv.at[wave, way, which],
+            src_ref=src,
+            dst_ref=dst.at[way],
+            send_sem=wave_send.at[way, which],
+            recv_sem=wave_recv.at[way, which],
             device_id=ways[way],
             device_id_type=MESH,
         )
 
-    def early_args(wave, way):
-        return (way, (way, 2, way)[wave]) if wave < 2 else (1 - way, way)
-
-    def start_wave(wave, parts=(0, 1)):
-        for way in range(2):
-            for which in parts:
-                copy = early_copy(wave, way, which, *early_args(wave, way))
-                copy.start()
-                sent.append(copy)
-
-    def await_wave(wave, way, parts=(0, 1)):
-        for which in parts:
-            early_copy(wave, way, which, *early_args(wave, way)).wait_recv()
-
-    start_wave(0)
-    start_wave(2)
-
+
+    for which in (0,):
+        for way in range(2):
+            copy = early_copy(way, which)
+            copy.start()
+            sent.append(copy)
     @pl.when(core == 1)
     def _():
         pl.semaphore_wait(barrier, 2 * ((ny - 1) + (nz - 1)))
@@ -214,6 +203,11 @@
     for k in range(2, 6):
         loads[k].wait()
     arrive(rs, col_peers, rs_recv, rs_send)
+    for which in (1,):
+        for way in range(2):
+            copy = early_copy(way, which)
+            copy.start()
+            sent.append(copy)
     full_rows = total(rs, n_col)
     old = vr[...]
     lane = lax.broadcasted_iota(jnp.int32, (1, 2 * rows), 1)
@@ -267,9 +261,6 @@
             copy.start()
             sent.append(copy)
 
-    for way in range(2):
-        await_wave(0, way, (0,))
-    start_wave(1, (0,))
     arrive(tt_z, z_peers, tz_recv, tz_send)
     tt = total(tt_z, nz)
     terms = tt[:, :cw] * inv_cols
@@ -282,9 +273,25 @@
     mean_at = jnp.sum(tt[:, cw + rows :], axis=1, keepdims=True) * (1.0 / n_rows)
     for k in range(8, 10):
         loads[k].wait()
-    for way in range(2):
-        await_wave(0, way, (1,))
-    start_wave(1, (1,))
+    def ahead_copy(way, which):
+        box = (far_a, far_g)[which]
+        rows_, cols_ = pl.ds(0, AHEAD), pl.ds(way * half, half)
+        return pltpu.make_async_remote_copy(
+            src_ref=box.at[way, rows_, cols_],
+            dst_ref=box.at[2, rows_, cols_],
+            send_sem=ahead_send.at[way, which],
+            recv_sem=ahead_recv.at[way, which],
+            device_id=ways[way],
+            device_id_type=MESH,
+        )
+
+    for which in range(2):
+        for way in range(2):
+            early_copy(way, which).wait_recv()
+            copy = ahead_copy(way, which)
+            copy.start()
+            sent.append(copy)
+
     arrive(sq, col_peers, sq_recv, sq_send)
     sums = total(sq, n_col)
     square_up = mean_up * (jnp.sum(sums[:, :128], axis=1, keepdims=True) * (1.0 / (n_rows * full_up)))
@@ -315,9 +322,9 @@
 
     scale_up = RATE * (1.0 - BETA) * clip_up * jnp.sqrt(mean_up)
 
-    def finish(a_ref, g_ref, roots, owner):
+    def finish(a_ref, g_ref, roots, owner, start, stop):
         scaled = roots * scale_up
-        for r0 in range(0, EARLY, 16):
+        for r0 in range(start, stop, 16):
             here = slice(r0, r0 + 16)
             move = g_ref[here, :].astype(F32) * root_up[here, :] * scaled
             cp_up[here, pl.ds(pl.multiple_of(owner * cu, cu), cu)] = (
@@ -383,11 +390,11 @@
             advance(up, r0, n)
         near(0, 0, i)
         near(1, 1, i)
+    for i in range(n_late):
+        near(0, 1, i)
+        near(1, 0, i)
         for up, r0, n in chunks[i]:
             to_sibling((up, r0, n, 0, cu if up else ca), col, 0)
-    advance(True, 0, EARLY, early=True)
-    finish(part_a, vg_up, col_box[0], col)
-    to_sibling((True, 0, EARLY, 0, cu), col, 0)
 
     lane4 = lax.broadcasted_iota(jnp.int32, (1, 128), 1)
     four = jnp.where(
@@ -404,28 +411,37 @@
                 device_id=x_devs[0], device_id_type=MESH,
             ).wait_recv()
 
-    def finish_box(box):
-        owner, column, waves = (
-            (left_col, 3, ((0, 0), (2, 0))), (right_col, 1, ((0, 1), (2, 1))), (across, 2, ((1, 0), (1, 1)))
-        )[box]
-        for wave, way in waves:
-            if wave:
-                await_wave(wave, way)
-        finish(far_a.at[box], far_g.at[box], col_box[column], owner)
-        to_sibling((True, 0, EARLY, 0, cu), owner, box + 1)
-
     from_cols = (left_col, right_col)
+    roots_of = (col_box[nx - 1], col_box[1])
+    marks = list(range(AHEAD, EARLY, RELAY))
+    for c, r0 in enumerate(marks):
+        for way in range(2):
+            finish(far_a.at[way], far_g.at[way], roots_of[way], from_cols[way], r0, r0 + RELAY)
+            push((True, r0, RELAY, way * half, half), from_cols[way], ways[way], far_send.at[way, 0], relay_recv.at[way, c])
+    for way in range(2):
+        finish(far_a.at[way], far_g.at[way], roots_of[way], from_cols[way], 0, AHEAD)
+        to_sibling((True, 0, EARLY, 0, cu), from_cols[way], way + 1)
+    advance(True, 0, EARLY, early=True)
+    finish(part_a, vg_up, col_box[0], col, 0, EARLY)
+    to_sibling((True, 0, EARLY, 0, cu), col, 0)
     for i in range(n_late):
-        if i < 3:
-            finish_box((2, 0, 1)[i])
         for way in range(2):
             unit, owner = units[way][i], from_cols[way]
             await_recv(view(unit, owner), near_recv.at[way, way, i])
             push(unit, owner, ways[way], far_send.at[way, kind(unit)], far_recv.at[way, i])
-            near(way, 1 - way, i)
             to_sibling(unit, owner, way + 1)
     for copy in sent:
         copy.wait_send()
+    for which in range(2):
+        for way in range(2):
+            ahead_copy(way, which).wait_recv()
+    finish(far_a.at[2], far_g.at[2], col_box[2], across, 0, AHEAD)
+    to_sibling((True, 0, AHEAD, 0, cu), across, 3)
+    for c, r0 in enumerate(marks):
+        for way in range(2):
+            unit = (True, r0, RELAY, way * half, half)
+            await_recv(view(unit, across), relay_recv.at[way, c])
+            to_sibling(unit, across, 3)
     for i in range(n_late):
         for way in range(2):
             unit = units[way][i]
@@ -442,7 +458,7 @@
             here = pl.ds(pl.multiple_of(col * w, w), w)
             await_send(ref.at[pl.ds(0, n), here], own_send.at[side, t])
             here = pl.ds(pl.multiple_of(col * w, w // 2), w // 2)
-            await_send(ref.at[pl.ds(0, n), here], far_send.at[side, t])
+            await_send(ref.at[pl.ds(0, (rows - AHEAD, rows)[t]), here], far_send.at[side, t])
     other = lambda c: c + 1 - 2 * core
     owners = [col, left_col, right_col, across]
     for k, owner in enumerate(owners):
@@ -494,7 +510,7 @@
         dma((max(nz - 1, 1),)), dma((nz,)),
         dma((n_col - 1,)), dma((n_col,)),
         dma((2, 2)), dma((2, 2, n_late)), dma((2, 2)), dma((2, n_late)), dma((4, 2)), dma((4, 2)),
-        dma((3, 2, 2)), dma((3, 2, 2)),
+        dma((2, 2)), dma((2, 2)), dma((2, 2)), dma((2, 2)), dma((2, (EARLY - AHEAD) // RELAY)),
         dma((nx,)), dma((nx,)),
         pltpu.SemaphoreType.REGULAR, pltpu.SemaphoreType.REGULAR,
     ]

time: 46.4 us -> 45.8 us (0.987)
  Pallas kernels: 45.6 us -> 45 us
    pallas_call x1, Pallas kernels: 42.5 us -> 41.9 us  [on_device(): pl.pallas_call(functools.partial(body, dims), out_shape=out_shape, in_spe...]
where the time goes in v4:
time: 45.8 us; the launch traced here: 45.7 us
  Pallas kernels  45 us (98%)
  between operations  0.66 us (1%)
    pallas_call x1, Pallas kernels, on_device(): pl.pallas_call(functools.partial(body, dims), out_shape=out_shape, in_spe...  41.9 us
    pallas_call x1, Pallas kernels, on_device(): pl.pallas_call(write_out, out_shape=[pltpu.HBM(o.shape, o.dtype) for o in...  3.11 us

profile of v4, /device:TPU:1, one launch (start us, length us, event | category | flops | bytes accessed | tf_op | source)
XLA Modules:
  0.0 45.7 jit_solution(4264145982333787706)
XLA Ops:
  0.6 41.9 %shard_map.185 = (f32[128,2048]{1,0:T(8,128)S(1)}, bf16[128,2048]{1,0:T(8,128)(2,1)S(1)}, f32[1,128]{1,0:T(1,128)S(1)}, f32[1,2048]{1,0:T(1,128)S(1)}, bf16[128,...) custom-call(f32[128,2048]{1,0:T(8,128)} %p_up.1, ...), custom_call_target="tpu_custom_call" | custom-call | flops 6553600 | bytes 3276800 | tf_op jit(solution)/shard_map/pallas_call | solution.py:526
  42.6 3.1 %shard_map.186 = (f32[128,2048]{1,0:T(8,128)}, bf16[128,2048]{1,0:T(8,128)(2,1)}, f32[1,128]{1,0:T(1,128)}, f32[1,2048]{1,0:T(1,128)}, bf16[128,16384]{1,0:T(8,1...) custom-call(f32[128,2048]{1,0:T(8,128)S(1)} %get-tuple-element.33.re, ...), custom_call_target="tpu_custom_call" | custom-call | bytes 7208960 | tf_op jit(solution)/shard_map/pallas_call | solution.py:547

commit v5 on v4

--- a/solution.py
+++ b/solution.py
@@ -391,8 +391,6 @@
         near(0, 0, i)
         near(1, 1, i)
     for i in range(n_late):
-        near(0, 1, i)
-        near(1, 0, i)
         for up, r0, n in chunks[i]:
             to_sibling((up, r0, n, 0, cu if up else ca), col, 0)
 
@@ -429,6 +427,7 @@
             unit, owner = units[way][i], from_cols[way]
             await_recv(view(unit, owner), near_recv.at[way, way, i])
             push(unit, owner, ways[way], far_send.at[way, kind(unit)], far_recv.at[way, i])
+            near(way, 1 - way, i)
             to_sibling(unit, owner, way + 1)
     for copy in sent:
         copy.wait_send()
@@ -474,6 +473,7 @@
         pltpu.make_async_copy(src, dst, sems.at[i])
         for i, (src, dst) in enumerate(zip(refs[:n], refs[n : 2 * n]))
     ]
+    copies.sort(key=lambda copy: -copy.src_ref.shape[1])
     for copy in copies:
         copy.start()
     for copy in copies:

time: 45.8 us -> 45.6 us (level)
  no operation moved by 1% of the time
where the time goes in v5:
time: 45.6 us; the launch traced here: 45.5 us
  Pallas kernels  44.8 us (98%)
  between operations  0.66 us (1%)
    pallas_call x1, Pallas kernels, on_device(): pl.pallas_call(functools.partial(body, dims), out_shape=out_shape, in_spe...  41.8 us
    pallas_call x1, Pallas kernels, on_device(): pl.pallas_call(write_out, out_shape=[pltpu.HBM(o.shape, o.dtype) for o in...  3.02 us

profile of v5, /device:TPU:1, one launch (start us, length us, event | category | flops | bytes accessed | tf_op | source)
XLA Modules:
  0.0 45.5 jit_solution(4401799077348128156)
XLA Ops:
  0.6 41.8 %shard_map.185 = (f32[128,2048]{1,0:T(8,128)S(1)}, bf16[128,2048]{1,0:T(8,128)(2,1)S(1)}, f32[1,128]{1,0:T(1,128)S(1)}, f32[1,2048]{1,0:T(1,128)S(1)}, bf16[128,...) custom-call(f32[128,2048]{1,0:T(8,128)} %p_up.1, ...), custom_call_target="tpu_custom_call" | custom-call | flops 6553600 | bytes 3276800 | tf_op jit(solution)/shard_map/pallas_call | solution.py:526
  42.5 3.0 %shard_map.186 = (f32[128,2048]{1,0:T(8,128)}, bf16[128,2048]{1,0:T(8,128)(2,1)}, f32[1,128]{1,0:T(1,128)}, f32[1,2048]{1,0:T(1,128)}, bf16[128,16384]{1,0:T(8,1...) custom-call(f32[128,2048]{1,0:T(8,128)S(1)} %get-tuple-element.33.re, ...), custom_call_target="tpu_custom_call" | custom-call | bytes 7208960 | tf_op jit(solution)/shard_map/pallas_call | solution.py:547
